TPU v7x, 128 devices: a whole 4x4x4 slice. The times are simulated.
128 devices in a mesh: fsdp: 4 (over z), seq: 8 (over x_hi, y), mp: 4 (over x_lo, core).
Axes of the slice: x: 4 (x_hi: 2, x_lo: 2; x = x_hi * 2 + x_lo), y: 4, z: 4, core: 2. Of those that a mesh axis runs over, the one named last changes fastest.
Arguments:
- inputs: float32 [16384, 2048], P(('fsdp', 'seq', 'mp')), may hold values from -6 to 6
- cotangent: float32 [16384, 2048], P(('fsdp', 'seq', 'mp')), may hold values from -24 to 24
- attn_weight: float32 [1, 128, 64, 2048], P(None, ('fsdp', 'seq', 'mp')), may hold values from -1 to 1
- expand_weight: float32 [1, 8192, 2048], P(None, ('fsdp', 'seq', 'mp')), may hold values from -0.125 to 0.125
- contract_weight: float32 [1, 8192, 2048], P(None, ('fsdp', 'seq', 'mp')), may hold values from -0.0625 to 0.0625
- norm_params: float32 [1, 2, 2048], P(None, None, ('fsdp', 'seq', 'mp')), may hold values from -0.3 to 1.3
- attn_moment: float32 [1, 128, 64, 2048], P(None, ('fsdp', 'seq', 'mp')), may hold values from -224 to 224
- expand_moment: float32 [1, 8192, 2048], P(None, ('fsdp', 'seq', 'mp')), may hold values from -224 to 224
- contract_moment: float32 [1, 8192, 2048], P(None, ('fsdp', 'seq', 'mp')), may hold values from -224 to 224
- norm_first: float32 [1, 2, 2048], P(None, None, ('fsdp', 'seq', 'mp')), may hold values from -80 to 80
- norm_second: float32 [1, 2, 2048], P(None, None, ('fsdp', 'seq', 'mp')), may hold values from 819.2 to 3276.8
Outputs:
- block_output: float32 [16384, 2048], P(('fsdp', 'seq', 'mp'))
- input_grad: float32 [16384, 2048], P(('fsdp', 'seq', 'mp'))
- attn_grad: float32 [1, 128, 64, 2048], P(None, ('fsdp', 'seq', 'mp'))
- attn_moment_next: float32 [1, 128, 64, 2048], P(None, ('fsdp', 'seq', 'mp'))
- attn_next: float32 [1, 128, 64, 2048], P(None, ('fsdp', 'seq', 'mp'))
- expand_grad: float32 [1, 8192, 2048], P(None, ('fsdp', 'seq', 'mp'))
- expand_moment_next: float32 [1, 8192, 2048], P(None, ('fsdp', 'seq', 'mp'))
- expand_next: float32 [1, 8192, 2048], P(None, ('fsdp', 'seq', 'mp'))
- contract_grad: float32 [1, 8192, 2048], P(None, ('fsdp', 'seq', 'mp'))
- contract_moment_next: float32 [1, 8192, 2048], P(None, ('fsdp', 'seq', 'mp'))
- contract_next: float32 [1, 8192, 2048], P(None, ('fsdp', 'seq', 'mp'))
- norm_grad: float32 [1, 2, 2048], P(None, None, ('fsdp', 'seq', 'mp'))
- norm_first_next: float32 [1, 2, 2048], P(None, None, ('fsdp', 'seq', 'mp'))
- norm_second_next: float32 [1, 2, 2048], P(None, None, ('fsdp', 'seq', 'mp'))
- norm_next: float32 [1, 2, 2048], P(None, None, ('fsdp', 'seq', 'mp'))
All inputs are finite; a program needn't handle non-finite values.
Results may differ from a plain program's by a relative error of at most 0.023.
Values may be sent and summed in bfloat16 or wider, within the bound.
A program may use at most 192 MiB of HBM per device.

v0:
```python
import math

import jax
import jax.numpy as jnp
from jax import lax
from jax.sharding import PartitionSpec as P

D = 2048
H = 32
HD = 64
ROT = 32
MAX_LEN = 2048
LAYERS = 1
NS_STEPS = 5
STEP = 10


eps_norm = 1e-05
rope_base = 10000.0
muon_beta = 0.95
muon_rate = 0.15
muon_decay = 0.01
polish_a = 3.4445
polish_b = -4.775
polish_c = 2.0315
adam_first = 0.9
adam_second = 0.95
adam_rate = 0.5
adam_eps = 1e-08
masked_score = -1e30
highest = lax.Precision.HIGHEST
across = (((1,), (1,)), ((), ()))
downward = (((0,), (0,)), ((), ()))


def angles(positions, half):
    freq = rope_base ** (-2.0 * jnp.arange(half, dtype=jnp.float32) / (2 * half))
    turned = positions[:, None] * freq[None, :]
    return (jnp.cos(turned)[:, None, :], jnp.sin(turned)[:, None, :])


def rotate(values, cosine, sine):
    half = cosine.shape[-1]
    first = values[..., :half]
    second = values[..., half : 2 * half]
    return jnp.concatenate(
        [first * cosine - second * sine, second * cosine + first * sine, values[..., 2 * half :]],
        axis=-1,
    )


def gelu(values):
    return jax.nn.gelu(values, approximate=True)


def causal(offset, block, width):
    rows_at = offset + lax.broadcasted_iota(jnp.int32, (block, width), 0)
    cols_at = lax.broadcasted_iota(jnp.int32, (block, width), 1)
    return (cols_at <= rows_at)[None]


def block_scores(query, keys, start, block, first):
    stop = start + block
    scores = jnp.einsum(
        "qhe,khe->hqk", query[start:stop], keys[first:stop], preferred_element_type=jnp.float32
    ) * HD ** (-0.5)
    return jnp.where(causal(start - first, block, stop - first), scores, masked_score)


def attend_forward(whole, heads, block, seq_len):
    length = whole.shape[0]
    query = whole[:, 0].reshape(length, heads, HD)
    keys = whole[:, 1].reshape(length, heads, HD)
    value = whole[:, 2].reshape(length, heads, HD)
    outputs = []
    totals = []
    for index in range(length // block):
        start = index * block
        stop = start + block
        first = start // seq_len * seq_len
        scores = block_scores(query, keys, start, block, first)
        top = jnp.max(scores, axis=-1, keepdims=True)
        expo = jnp.exp(scores - top)
        total = jnp.sum(expo, axis=-1, keepdims=True)
        probs = (expo / total).astype(jnp.bfloat16)
        attended = jnp.einsum(
            "hqk,khe->qhe", probs, value[first:stop], preferred_element_type=jnp.float32
        )
        outputs.append(attended.astype(jnp.bfloat16).reshape(block, heads * HD))
        totals.append(top + jnp.log(total))
    return (jnp.concatenate(outputs, axis=0), totals)


def attend_backward(whole, totals, grad_attended, heads, block, seq_len):
    length = whole.shape[0]
    scale = HD ** (-0.5)
    query = whole[:, 0].reshape(length, heads, HD)
    keys = whole[:, 1].reshape(length, heads, HD)
    value = whole[:, 2].reshape(length, heads, HD)
    grad_out = grad_attended.reshape(length, heads, HD)
    grad_query = []
    grad_keys = jnp.zeros((length, heads, HD), jnp.float32)
    grad_value = jnp.zeros((length, heads, HD), jnp.float32)
    for index in range(length // block):
        start = index * block
        stop = start + block
        first = start // seq_len * seq_len
        scores = block_scores(query, keys, start, block, first)
        probs_full = jnp.exp(scores - totals[index])
        probs = probs_full.astype(jnp.bfloat16)
        grad_block = grad_out[start:stop]
        grad_value = grad_value.at[first:stop].add(
            jnp.einsum("hqk,qhe->khe", probs, grad_block, preferred_element_type=jnp.float32)
        )
        grad_probs = jnp.einsum(
            "qhe,khe->hqk", grad_block, value[first:stop], preferred_element_type=jnp.float32
        )
        inner = jnp.sum(probs_full * grad_probs, axis=-1, keepdims=True)
        grad_scores = (probs_full * (grad_probs - inner)).astype(jnp.bfloat16)
        grad_query.append(
            (
                jnp.einsum(
                    "hqk,khe->qhe",
                    grad_scores,
                    keys[first:stop],
                    preferred_element_type=jnp.float32,
                )
                * scale
            ).astype(jnp.bfloat16)
        )
        grad_keys = grad_keys.at[first:stop].add(
            jnp.einsum(
                "hqk,qhe->khe", grad_scores, query[start:stop], preferred_element_type=jnp.float32
            )
            * scale
        )
    stacked = [
        jnp.concatenate(grad_query, axis=0),
        grad_keys.astype(jnp.bfloat16),
        grad_value.astype(jnp.bfloat16),
    ]
    return jnp.stack([piece.reshape(length, heads * HD) for piece in stacked], axis=1)


def polish(moment):
    size = jnp.sqrt(jnp.sum(moment * moment, axis=(1, 2), keepdims=True)) + 1e-07
    current = moment / size
    for turn in range(NS_STEPS):
        gram = jnp.einsum("bij,bkj->bik", current, current, precision=highest)
        mixed = polish_b * gram + polish_c * jnp.einsum(
            "bij,bjk->bik", gram, gram, precision=highest
        )
        current = polish_a * current + jnp.einsum("bij,bjk->bik", mixed, current, precision=highest)
    return current


def muon_step(weight, grad, moment):
    moment_next = muon_beta * moment + grad
    ortho = polish(moment_next.reshape(-1, HD, D)).reshape(moment.shape)
    return (moment_next, weight - muon_rate * (muon_decay * weight + 0.2 * math.sqrt(D) * ortho))


def body(
    inputs,
    cotangent,
    attn_weight,
    expand_weight,
    contract_weight,
    norm_params,
    attn_moment,
    expand_moment,
    contract_moment,
    norm_first,
    norm_second,
):
    seq_count = lax.axis_size("seq")
    mp_count = lax.axis_size("mp")
    rows = inputs.shape[0]
    group_rows = rows * mp_count
    length = group_rows * seq_count
    seq_len = min(MAX_LEN, length)
    local_heads = H // mp_count
    heads = local_heads // seq_count
    block = min(512, seq_len)
    places = lax.axis_index("seq") * group_rows + jnp.arange(group_rows, dtype=jnp.int32)
    positions = (places % seq_len).astype(jnp.float32)
    cosine, sine = angles(positions, ROT // 2)
    whole_norm_rows = lax.all_gather(norm_params, ("fsdp", "seq", "mp"), axis=2, tiled=True)
    state = inputs
    layer_module = 0
    attn_w = lax.all_gather(
        attn_weight[layer_module].astype(jnp.bfloat16), ("fsdp", "seq"), axis=0, tiled=True
    )
    expand_w = lax.all_gather(
        expand_weight[layer_module].astype(jnp.bfloat16), ("fsdp", "seq"), axis=0, tiled=True
    )
    contract_w = lax.all_gather(
        contract_weight[layer_module].astype(jnp.bfloat16), ("fsdp", "seq"), axis=0, tiled=True
    )
    qkv_w = attn_w[: 3 * local_heads].reshape(3 * local_heads * HD, D)
    out_w = attn_w[3 * local_heads :].reshape(local_heads * HD, D)
    feature_mean = jnp.mean(state, axis=-1, keepdims=True)
    centered_input = state - feature_mean
    inverse_deviation = lax.rsqrt(
        jnp.mean(centered_input * centered_input, axis=-1, keepdims=True) + eps_norm
    )
    normed = (
        centered_input * inverse_deviation * whole_norm_rows[layer_module, 0]
        + whole_norm_rows[layer_module, 1]
    ).astype(jnp.bfloat16)
    group = lax.all_gather(normed, "mp", axis=0, tiled=True)
    lin = lax.dot_general(group, qkv_w, across, preferred_element_type=jnp.float32).reshape(
        group_rows, 3, local_heads, HD
    )
    query = rotate(lin[:, 0], cosine, sine).astype(jnp.bfloat16)
    keys = rotate(lin[:, 1], cosine, sine).astype(jnp.bfloat16)
    value = lin[:, 2].astype(jnp.bfloat16)
    stacked = jnp.stack([query, keys, value], axis=1).reshape(group_rows, 3, local_heads * HD)
    whole = lax.all_to_all(stacked, "seq", split_axis=2, concat_axis=0, tiled=True)
    attended, totals = attend_forward(whole, heads, block, seq_len)
    back = lax.all_to_all(attended, "seq", split_axis=0, concat_axis=1, tiled=True)
    attn_part = jnp.dot(back, out_w, preferred_element_type=jnp.float32)
    upward = lax.dot_general(group, expand_w, across, preferred_element_type=jnp.float32)
    active = gelu(upward).astype(jnp.bfloat16)
    mlp_part = jnp.dot(active, contract_w, preferred_element_type=jnp.float32)
    branch = lax.psum_scatter(
        (attn_part + mlp_part).astype(jnp.bfloat16), "mp", scatter_dimension=0, tiled=True
    ).astype(jnp.float32)
    saved = [
        (
            centered_input,
            inverse_deviation,
            group,
            whole,
            totals,
            back,
            upward,
            active,
            qkv_w,
            out_w,
            expand_w,
            contract_w,
        )
    ]
    state = state + branch
    grad_state = cotangent
    norm_parts = [None] * LAYERS
    updates = [None] * LAYERS
    for layer_module in reversed(range(LAYERS)):
        (
            centered_input,
            inverse_deviation,
            group,
            whole,
            totals,
            back,
            upward,
            active,
            qkv_w,
            out_w,
            expand_w,
            contract_w,
        ) = saved[layer_module]
        grad_branch = grad_state.astype(jnp.bfloat16)
        grad_group = lax.all_gather(grad_branch, "mp", axis=0, tiled=True)
        grad_active = lax.dot_general(
            grad_group, contract_w, across, preferred_element_type=jnp.float32
        )
        slope = jax.vjp(gelu, upward)[1]
        grad_up = slope(grad_active)[0].astype(jnp.bfloat16)
        contract_part = lax.dot_general(
            active, grad_group, downward, preferred_element_type=jnp.float32
        )
        expand_part = lax.dot_general(grad_up, group, downward, preferred_element_type=jnp.float32)
        grad_normed = jnp.dot(grad_up, expand_w, preferred_element_type=jnp.float32)
        grad_back = lax.dot_general(
            grad_group, out_w, across, preferred_element_type=jnp.float32
        ).astype(jnp.bfloat16)
        out_part = lax.dot_general(back, grad_group, downward, preferred_element_type=jnp.float32)
        grad_attended = lax.all_to_all(grad_back, "seq", split_axis=1, concat_axis=0, tiled=True)
        grad_whole = attend_backward(whole, totals, grad_attended, heads, block, seq_len)
        grad_stack = lax.all_to_all(grad_whole, "seq", split_axis=0, concat_axis=2, tiled=True)
        grad_query = rotate(
            grad_stack[:, 0].reshape(group_rows, local_heads, HD).astype(jnp.float32), cosine, -sine
        ).astype(jnp.bfloat16)
        grad_keys = rotate(
            grad_stack[:, 1].reshape(group_rows, local_heads, HD).astype(jnp.float32), cosine, -sine
        ).astype(jnp.bfloat16)
        grad_value = grad_stack[:, 2].reshape(group_rows, local_heads, HD)
        grad_lin = jnp.stack([grad_query, grad_keys, grad_value], axis=1).reshape(
            group_rows, 3 * local_heads * HD
        )
        qkv_part = lax.dot_general(grad_lin, group, downward, preferred_element_type=jnp.float32)
        grad_normed = grad_normed + jnp.dot(grad_lin, qkv_w, preferred_element_type=jnp.float32)
        attn_part_grad = jnp.concatenate([qkv_part, out_part], axis=0).reshape(
            4 * local_heads, HD, D
        )
        attn_share, expand_share, contract_share = (
            lax.psum_scatter(
                attn_part_grad.astype(jnp.bfloat16),
                ("fsdp", "seq"),
                scatter_dimension=0,
                tiled=True,
            ).astype(jnp.float32),
            lax.psum_scatter(
                expand_part.astype(jnp.bfloat16), ("fsdp", "seq"), scatter_dimension=0, tiled=True
            ).astype(jnp.float32),
            lax.psum_scatter(
                contract_part.astype(jnp.bfloat16), ("fsdp", "seq"), scatter_dimension=0, tiled=True
            ).astype(jnp.float32),
        )
        hidden_gradient = lax.psum_scatter(
            grad_normed.astype(jnp.bfloat16), "mp", scatter_dimension=0, tiled=True
        ).astype(jnp.float32)
        normalized_input = centered_input * inverse_deviation
        norm_parts[layer_module] = jnp.stack(
            [jnp.sum(hidden_gradient * normalized_input, axis=0), jnp.sum(hidden_gradient, axis=0)],
            axis=0,
        )
        normalized_input_gradient = hidden_gradient * whole_norm_rows[layer_module, 0]
        grad_state = grad_state + inverse_deviation * (
            normalized_input_gradient
            - jnp.mean(normalized_input_gradient, axis=-1, keepdims=True)
            - normalized_input
            * jnp.mean(normalized_input_gradient * normalized_input, axis=-1, keepdims=True)
        )
        attn_mom, attn_new = muon_step(
            attn_weight[layer_module], attn_share, attn_moment[layer_module]
        )
        expand_mom, expand_new = muon_step(
            expand_weight[layer_module], expand_share, expand_moment[layer_module]
        )
        contract_mom, contract_new = muon_step(
            contract_weight[layer_module], contract_share, contract_moment[layer_module]
        )
        updates[layer_module] = (
            attn_share,
            attn_mom,
            attn_new,
            expand_share,
            expand_mom,
            expand_new,
            contract_share,
            contract_mom,
            contract_new,
        )
    norm_share = lax.psum_scatter(
        jnp.stack(norm_parts, axis=0), ("fsdp", "seq", "mp"), scatter_dimension=2, tiled=True
    )
    first_next = adam_first * norm_first + (1.0 - adam_first) * norm_share
    second_next = adam_second * norm_second + (1.0 - adam_second) * norm_share * norm_share
    first_fix = 1.0 - adam_first**STEP
    second_fix = 1.0 - adam_second**STEP
    norm_next = norm_params - adam_rate * (first_next / first_fix) / (
        jnp.sqrt(second_next / second_fix) + adam_eps
    )
    stacked_out = [jnp.stack([updates[0][member]], axis=0) for member in range(9)]
    return (
        state,
        grad_state,
        stacked_out[0],
        stacked_out[1],
        stacked_out[2],
        stacked_out[3],
        stacked_out[4],
        stacked_out[5],
        stacked_out[6],
        stacked_out[7],
        stacked_out[8],
        norm_share,
        first_next,
        second_next,
        norm_next,
    )


def solution(mesh):
    return jax.shard_map(
        body,
        mesh=mesh,
        in_specs=(
            P(("fsdp", "seq", "mp"), None),
            P(("fsdp", "seq", "mp"), None),
            P(None, ("fsdp", "seq", "mp"), None, None),
            P(None, ("fsdp", "seq", "mp"), None),
            P(None, ("fsdp", "seq", "mp"), None),
            P(None, None, ("fsdp", "seq", "mp")),
            P(None, ("fsdp", "seq", "mp"), None, None),
            P(None, ("fsdp", "seq", "mp"), None),
            P(None, ("fsdp", "seq", "mp"), None),
            P(None, None, ("fsdp", "seq", "mp")),
            P(None, None, ("fsdp", "seq", "mp")),
        ),
        out_specs=(
            P(("fsdp", "seq", "mp"), None),
            P(("fsdp", "seq", "mp"), None),
            P(None, ("fsdp", "seq", "mp"), None, None),
            P(None, ("fsdp", "seq", "mp"), None, None),
            P(None, ("fsdp", "seq", "mp"), None, None),
            P(None, ("fsdp", "seq", "mp"), None),
            P(None, ("fsdp", "seq", "mp"), None),
            P(None, ("fsdp", "seq", "mp"), None),
            P(None, ("fsdp", "seq", "mp"), None),
            P(None, ("fsdp", "seq", "mp"), None),
            P(None, ("fsdp", "seq", "mp"), None),
            P(None, None, ("fsdp", "seq", "mp")),
            P(None, None, ("fsdp", "seq", "mp")),
            P(None, None, ("fsdp", "seq", "mp")),
            P(None, None, ("fsdp", "seq", "mp")),
        ),
        check_vma=False,
    )
```

profile of v0, /device:TPU:0, one launch (start us, length us, event | category | flops | bytes accessed | tf_op | source)
XLA Modules:
  0.0 1912.9 jit_solution(2462214261400440180)
XLA Ops:
  11.3 197.0 %all_gather.18 = f32[1,2,2048]{1,0,2:T(1,128)S(1)} all-gather(f32[1,2,16]{1,0,2:T(1,128)S(1)} %copy.42), channel_id=1, replica_groups=mesh['fsdp'=4,'seq'=8,'mp'=4] {'fsdp','seq','mp'}, dimensions={2}, use_global_device_ids=true | all-gather | bytes 16512 | tf_op jit(solution)/shard_map/all_gather | solution.py:188
  208.6 33.0 %slice_reduce_fusion.1 = (f32[2048]{0:T(1024)S(1)}, f32[2048]{0:T(1024)S(1)}) fusion(f32[1,2,2048]{1,0,2:T(1,128)S(1)} %all_gather.18), kind=kLoop, calls=%fused_computation.285 | loop fusion | bytes 32768 | tf_op jit(solution)/shard_map/slice | solution.py:208
  246.6 6.8 slice.694
  253.4 12.5 all-gather.8.cloned.1.call-done
  265.9 6.2 fusion.72
  279.7 6.4 all-to-all-start
  286.1 22.2 %all-gather.12.cloned.1.call-done = bf16[512,2048]{1,0:T(8,128)(2,1)} async-done(((bf16[128,2048]{1,0:T(8,128)(2,1)}), bf16[512,2048]{1,0:T(8,128)(2,1)}) %all-gather.12.cloned.1.call-update) | async-done | bytes 2097168 | tf_op jit(solution)/shard_map/all_gather | solution.py:265
  311.9 105.1 %all-gather.14.cloned.1.call-done = bf16[1,2048,2048]{2,1,0:T(8,128)(2,1)} async-done(((bf16[1,64,2048]{2,1,0:T(8,128)(2,1)}), bf16[1,2048,2048]{2,1,0:T(8,128)(2,1)}) %all-gather.14.cloned.1.call-update) | async-done | bytes 8388624 | tf_op jit(solution)/shard_map/all_gather | solution.py:194
  417.0 10.5 fusion.6
  434.9 7.4 all-to-all-done.2
  480.5 6.4 copy.49
  486.8 7.3 reshape.1877
  498.5 37.7 %all-gather.16.cloned.1.call-done = bf16[1,2048,2048]{2,1,0:T(8,128)(2,1)} async-done(((bf16[1,64,2048]{2,1,0:T(8,128)(2,1)}), bf16[1,2048,2048]{2,1,0:T(8,128)(2,1)}) %all-gather.16.cloned.1.call-update) | async-done | bytes 8388624 | tf_op jit(solution)/shard_map/all_gather | solution.py:197
  536.2 13.2 fusion.14
  556.0 7.3 reshape.1878
  563.3 6.7 copy.50
  603.6 11.5 fusion.2
  628.5 11.2 convolution_convert_fusion
  641.3 8.4 convolution_convert_fusion.1
  658.7 7.6 pad_maximum_fusion
  670.6 622.9 %reduce-scatter.19.cloned.1.call-done = f32[16,2]{1,0:T(8,128)} async-done(((f32[2048,2]{1,0:T(8,128)}), f32[16,2]{1,0:T(8,128)}) %reduce-scatter.19.cloned.1.call-update) | async-done | bytes 144
  1294.9 197.4 %reduce-scatter.17.cloned.1.call-done = bf16[64,2048]{1,0:T(8,128)(2,1)} async-done(((bf16[2048,2048]{1,0:T(8,128)(2,1)}), bf16[64,2048]{1,0:T(8,128)(2,1)}) %reduce-scatter.17.cloned.1.call-update) | async-done | bytes 262160 | tf_op jit(solution)/shard_map/reduce_scatter | solution.py:308
  1495.5 197.2 %reduce-scatter.15.cloned.1.call-done = bf16[64,2048]{1,0:T(8,128)(2,1)} async-done(((bf16[2048,2048]{1,0:T(8,128)(2,1)}), bf16[64,2048]{1,0:T(8,128)(2,1)}) %reduce-scatter.15.cloned.1.call-update) | async-done | bytes 262160 | tf_op jit(solution)/shard_map/reduce_scatter | solution.py:305
  1713.3 180.0 %reduce-scatter.13.cloned.1.call-done = bf16[1,64,2048]{2,1,0:T(8,128)(2,1)} async-done(((bf16[32,64,2048]{2,1,0:T(8,128)(2,1)}), bf16[1,64,2048]{2,1,0:T(8,128)(2,1)}) %reduce-scatter.13.cloned.1.call-update) | async-done | bytes 262160 | tf_op jit(solution)/shard_map/reduce_scatter | solution.py:299
  (324 shorter events, 173.6 us)
Async XLA Ops:
  7.2 201.1 %copy-start.9 = (f32[128,2048]{1,0:T(8,128)S(1)}, f32[128,2048]{1,0:T(8,128)}, u32[]{:S(2)}) copy-start(f32[128,2048]{1,0:T(8,128)} %param.43) | copy-start | bytes 3145732
  7.2 239.4 %all-gather.10.cloned.1.call-start = ((), (), s32[]{:S(2)}) async-start(), calls=%async_computation.11 | async-start | bytes 8650752 | tf_op jit(solution)/shard_map/all_gather | solution.py:191
  9.1 256.8 %all-gather.8.cloned.1.call-start = ((), (), s32[]{:S(2)}) async-start(), calls=%async_computation.10 | async-start | bytes 2621440 | tf_op jit(solution)/shard_map/all_gather | solution.py:211
  208.6 35.2 %copy-start.23 = (f32[128,2048]{1,0:T(8,128)S(1)}, f32[128,2048]{1,0:T(8,128)}, u32[]{:S(2)}) copy-start(f32[128,2048]{1,0:T(8,128)} %param.44) | copy-start | bytes 3145732
  243.2 65.1 %all-gather.12.cloned.1.call-start = ((), (), s32[]{:S(2)}) async-start(), calls=%async_computation.13 | async-start | bytes 2621440 | tf_op jit(solution)/shard_map/all_gather | solution.py:265
  244.6 172.4 %all-gather.14.cloned.1.call-start = ((), (), s32[]{:S(2)}) async-start(), calls=%async_computation.18 | async-start | bytes 8650752 | tf_op jit(solution)/shard_map/all_gather | solution.py:194
  245.4 290.7 %all-gather.16.cloned.1.call-start = ((), (), s32[]{:S(2)}) async-start(), calls=%async_computation.19 | async-start | bytes 8650752 | tf_op jit(solution)/shard_map/all_gather | solution.py:197
  279.7 147.9 %all-to-all-start = ((bf16[512,3,512]{0,1,2:T(4,128)(2,1)}), bf16[512,3,512]{0,1,2:T(4,128)(2,1)}, u32[]{:S(2)}, u32[]{:S(2)}) async-start(bf16[512,3,512]{0,1,2:T(4,128)(2,1)} %pad_maximum_fusion.1), calls=%async_computation | async-start | bytes 4194304 | tf_op jit(solution)/shard_map/all_to_all | solution.py:219
  427.5 14.8 all-to-all-start.2
  494.1 61.9 %all-to-all-start.3 = ((bf16[8,2,49152]{2,1,0:T(2,128)(2,1)}), bf16[8,2,49152]{2,1,0:T(2,128)(2,1)}, u32[]{:S(2)}, u32[]{:S(2)}) async-start(bf16[8,2,49152]{2,1,0:T(2,128)(2,1)} %reshape.1877), calls=%async_computation.4 | async-start | bytes 3145728 | tf_op jit(solution)/shard_map/all_to_all | solution.py:282
  498.4 125.6 %reduce-scatter.11.cloned.1.call-start = ((), (), s32[]{:S(2)}) async-start(), calls=%async_computation.14 | async-start | bytes 2621440 | tf_op jit(solution)/shard_map/reduce_scatter | solution.py:312
  600.1 18.0 all-to-all-start.1
  603.6 62.9 %reduce-scatter.9.cloned.1.call-start = ((), (), s32[]{:S(2)}) async-start(), calls=%async_computation.12 | async-start | bytes 2621440 | tf_op jit(solution)/shard_map/reduce_scatter | solution.py:226
  623.8 669.7 %reduce-scatter.19.cloned.1.call-start = ((), (), s32[]{:S(2)}) async-start(), calls=%async_computation.20 | async-start | bytes 1056768
  628.4 863.9 %reduce-scatter.17.cloned.1.call-start = ((), (), s32[]{:S(2)}) async-start(), calls=%async_computation.17 | async-start | bytes 8650752 | tf_op jit(solution)/shard_map/reduce_scatter | solution.py:308
  639.7 1053.0 %reduce-scatter.15.cloned.1.call-start = ((), (), s32[]{:S(2)}) async-start(), calls=%async_computation.16 | async-start | bytes 8650752 | tf_op jit(solution)/shard_map/reduce_scatter | solution.py:305
  649.7 1243.6 %reduce-scatter.13.cloned.1.call-start = ((), (), s32[]{:S(2)}) async-start(), calls=%async_computation.15 | async-start | bytes 8650752 | tf_op jit(solution)/shard_map/reduce_scatter | solution.py:299
  666.4 627.9 %copy-start.47 = (f32[1,2,16]{2,1,0:T(2,128)S(1)}, f32[1,2,16]{2,1,0:T(2,128)}, u32[]{:S(2)}) copy-start(f32[1,2,16]{2,1,0:T(2,128)} %param.48) | copy-start | bytes 388
  666.4 627.9 %copy-start.49 = (f32[1,2,16]{2,1,0:T(2,128)S(1)}, f32[1,2,16]{2,1,0:T(2,128)}, u32[]{:S(2)}) copy-start(f32[1,2,16]{2,1,0:T(2,128)} %param.53) | copy-start | bytes 388
  666.4 627.9 %copy-start.50 = (f32[1,2,16]{2,1,0:T(2,128)S(1)}, f32[1,2,16]{2,1,0:T(2,128)}, u32[]{:S(2)}) copy-start(f32[1,2,16]{2,1,0:T(2,128)} %param.52) | copy-start | bytes 388
  666.4 825.9 %copy-start.37 = (f32[1,64,2048]{2,1,0:T(8,128)S(1)}, f32[1,64,2048]{2,1,0:T(8,128)}, u32[]{:S(2)}) copy-start(f32[1,64,2048]{2,1,0:T(8,128)} %param.51) | copy-start | bytes 1572868
  1294.3 402.3 %copy-start.48 = (f32[1,2,16]{2,1,0:T(2,128)}, f32[1,2,16]{2,1,0:T(2,128)S(1)}, u32[]{:S(2)}) copy-start(f32[1,2,16]{2,1,0:T(2,128)S(1)} %copy.53) | copy-start | bytes 388
  1492.3 203.7 %copy-start.35 = (bf16[64,2048]{1,0:T(8,128)(2,1)S(1)}, bf16[64,2048]{1,0:T(8,128)(2,1)}, u32[]{:S(2)}) copy-start(bf16[64,2048]{1,0:T(8,128)(2,1)} %reduce-scatter.17.cloned.1.call-done) | copy-start | bytes 786436
  1708.4 184.8 %copy-start.39 = (f32[1,1,64,2048]{3,2,1,0:T(8,128)S(1)}, f32[1,1,64,2048]{3,2,1,0:T(8,128)}, u32[]{:S(2)}) copy-start(f32[1,1,64,2048]{3,2,1,0:T(8,128)} %param.49) | copy-start | bytes 1572868
  (48 other events, 302.2 us)
Sparse Core Ops, SparseCore 0:
  11.8 108.7 all-gather.9
  243.3 22.4 all-gather.7
  268.1 40.1 all-gather.11
  311.9 105.0 all-gather.13
  420.6 115.5 all-gather.15
  585.2 29.7 reduce-scatter.10
  623.9 26.9 reduce-scatter.8
  653.2 640.2 reduce-scatter.18
  1296.0 196.2 reduce-scatter.16
  1494.7 197.9 reduce-scatter.14
  1695.2 198.0 reduce-scatter.12
where the time goes:
time: 1920 us; the launch traced here: 1910 us
  waiting for transfers between devices  1390 us (72%)
  blocking collectives  197 us (10%)
  matrix products  160 us (8%)
  local copies, waits for them, and re-layouts  87.7 us (5%)
  other arithmetic  46.1 us (2%)
    unnamed x12, waiting for transfers between devices  623 us
    reduce_scatter x1, waiting for transfers between devices, body(): lax.psum_scatter(contract_part.astype(jnp.bfloat16), ('fsdp', 'seq'), sca...  197 us
    reduce_scatter x1, waiting for transfers between devices, body(): lax.psum_scatter(expand_part.astype(jnp.bfloat16), ('fsdp', 'seq'), scatt...  197 us
    all_gather x1, blocking collectives, body(): lax.all_gather(norm_params, ('fsdp', 'seq', 'mp'), axis=2, tiled=True)  197 us
    reduce_scatter x1, waiting for transfers between devices, body(): lax.psum_scatter(attn_part_grad.astype(jnp.bfloat16), ('fsdp', 'seq'), sc...  180 us
    all_gather x1, waiting for transfers between devices, body(): lax.all_gather(expand_weight[layer_module].astype(jnp.bfloat16), ('fsdp',...  105 us
  transfers between devices with their start and end apart: 15, of which 10 were waited for; matrix products, arithmetic and copies ran while one was open for 13% of the time, Pallas kernels for 0%

commit v1 on v0

v1 whole, which is shorter than its diff:
```python
import functools
import math

import jax
import jax.numpy as jnp
from jax import lax
from jax.experimental import pallas as pl
from jax.experimental.pallas import tpu as pltpu
from jax.sharding import PartitionSpec as P

D = 2048
H = 32
HD = 64
ROT = 32
LENGTH = 2048
NS_STEPS = 5
STEP = 10
ROWS = 128
WROWS = 64
KINDS = 3
QKV = 384
HIDDEN = 512
FIRST = QKV + HIDDEN
SECOND = 128 + HIDDEN
WALL = FIRST + SECOND

eps_norm = 1e-05
rope_base = 10000.0
muon_beta = 0.95
muon_rate = 0.15
muon_decay = 0.01
polish_a = 3.4445
polish_b = -4.775
polish_c = 2.0315
adam_first = 0.9
adam_second = 0.95
adam_rate = 0.5
adam_eps = 1e-08
masked_score = -1e30
highest = lax.Precision.HIGHEST
across = (((1,), (1,)), ((), ()))
downward = (((0,), (0,)), ((), ()))
MESH = pl.DeviceIdType.MESH
f32 = jnp.float32
bf16 = jnp.bfloat16


def place():
    z = lax.axis_index("fsdp")
    s = lax.axis_index("seq")
    m = lax.axis_index("mp")
    return z, s // 4, lax.rem(s, 4), m // 2, lax.rem(m, 2)


def device(z, xh, y, xl, c):
    return (lax.rem(z + 4, 4), xh * 4 + lax.rem(y + 4, 4), xl * 2 + c)


def token_rows(y, xl, c, start=0, size=ROWS):
    block = lax.rem(y + 4, 4) * 4 + xl * 2 + c
    return pl.ds(pl.multiple_of(block * ROWS + start, 64), size)


def weight_rows(kind, z, xh, start=0, size=WROWS):
    z = lax.rem(z + 4, 4)
    if kind == 0:
        base = z * 128 + (z // 3) * HIDDEN + xh * 64
    elif kind == 1:
        base = QKV + z * 128 + xh * 64
    else:
        base = FIRST + 128 + z * 128 + xh * 64
    return pl.ds(pl.multiple_of(base + start, 32), size)


class Net:
    def __init__(self, send, recv):
        self.send, self.recv, self.used, self.sent = send, recv, 0, []

    def go(self, src, dst, peer):
        slot = self.used
        self.used += 1
        copy = pltpu.make_async_remote_copy(
            src_ref=src,
            dst_ref=dst,
            send_sem=self.send.at[slot],
            recv_sem=self.recv.at[slot],
            device_id=peer,
            device_id_type=MESH,
        )
        copy.start()
        self.sent.append(copy)
        return copy

    def drain(self):
        for copy in self.sent:
            copy.wait_send()
        self.sent = []


class Local:
    def __init__(self, sems):
        self.sems, self.used = sems, 0

    def go(self, src, dst):
        copy = pltpu.make_async_copy(src, dst, self.sems.at[self.used])
        self.used += 1
        copy.start()
        return copy


def greet(peers):
    barrier = pltpu.get_barrier_semaphore()
    for peer in peers:
        pl.semaphore_signal(barrier, inc=1, device_id=peer, device_id_type=MESH)
    pl.semaphore_wait(barrier, len(peers))


def stage_peers(at):
    z, xh, y, xl, c = at
    return [
        [device(z + k, xh, y, xl, c) for k in (1, 2, 3)],
        [device(z, xh, y + k, xl, c) for k in (1, 2, 3)],
        [
            device(z, xh, y, 1 - xl, c),
            device(z, 1 - xh, y, xl, c),
            device(z, 1 - xh, y, 1 - xl, c),
        ],
        [device(z, xh, y, xl, 1 - c)],
    ]


def staged_sum(net, stages, sums, landed, between=None):
    slot = 0
    for stage, peers in enumerate(stages):
        copies = [
            net.go(sums.at[stage], landed.at[slot + k], peer) for k, peer in enumerate(peers)
        ]
        if between is not None:
            between(stage)
        total = sums[stage]
        for k, copy in enumerate(copies):
            copy.wait_recv()
            total = total + landed[slot + k]
        sums[stage + 1] = total
        slot += len(peers)


def spread(flat):
    gain = jnp.concatenate([flat[k : k + 1] for k in range(4)], axis=1)
    bias = jnp.concatenate([flat[k : k + 1] for k in range(4, 8)], axis=1)
    return gain, bias


class TokenGather:
    def __init__(self, net, at, full):
        self.net, self.at, self.full = net, at, full
        z, xh, y, xl, c = at
        self.xpart = device(z, xh, y, 1 - xl, c)
        self.yp = device(z, xh, y + 1, xl, c)
        self.ym = device(z, xh, y - 1, xl, c)
        self.sib = device(z, xh, y, xl, 1 - c)
        self.sibs = []

    def rows(self, dy, dx, start=0, size=ROWS):
        z, xh, y, xl, c = self.at
        return self.full.at[token_rows(y + dy, xl if dx == 0 else 1 - xl, c, start, size)]

    def own(self, block):
        go, here = self.net.go, self.rows(0, 0)
        self.l = go(block, here, self.yp)
        self.r = go(block, here, self.ym)
        self.p = go(block, here, self.xpart)
        self.sibs.append(go(block, here, self.sib))

    def share(self, dy, dx):
        self.sibs.append(self.net.go(self.rows(dy, dx), self.rows(dy, dx), self.sib))

    def near(self):
        go = self.net.go
        self.l.wait_recv()
        half = self.rows(-1, 0, 0, 64)
        self.a = go(half, half, self.yp)
        self.r.wait_recv()
        half = self.rows(1, 0, 64, 64)
        self.b = go(half, half, self.ym)
        self.p.wait_recv()
        other = self.rows(0, 1)
        self.lp = go(other, other, self.yp)
        self.rp = go(other, other, self.ym)
        self.share(-1, 0)
        self.share(1, 0)
        self.share(0, 1)

    def far(self):
        self.a.wait_recv()
        self.b.wait_recv()
        opposite = self.rows(2, 0)
        self.xo = self.net.go(opposite, opposite, self.xpart)
        self.share(2, 0)

    def rest(self):
        self.lp.wait_recv()
        self.share(-1, 1)
        self.rp.wait_recv()
        self.share(1, 1)
        self.xo.wait_recv()
        self.share(2, 1)

    def end(self):
        for copy in self.sibs:
            copy.wait_recv()


class WeightGather:
    def __init__(self, net, at, full, kind):
        self.net, self.at, self.full, self.kind = net, at, full, kind
        z, xh, y, xl, c = at
        self.hpart = device(z, 1 - xh, y, xl, c)
        self.zp = device(z + 1, xh, y, xl, c)
        self.zm = device(z - 1, xh, y, xl, c)

    def rows(self, dz, dh, start=0, size=WROWS):
        z, xh = self.at[:2]
        return self.full.at[
            weight_rows(self.kind, z + dz, xh if dh == 0 else 1 - xh, start, size)
        ]

    def own(self, block):
        go, here = self.net.go, self.rows(0, 0)
        self.l = go(block, here, self.zp)
        self.r = go(block, here, self.zm)
        self.p = go(block, here, self.hpart)

    def near(self):
        go = self.net.go
        self.l.wait_recv()
        half = self.rows(-1, 0, 0, 32)
        self.a = go(half, half, self.zp)
        self.r.wait_recv()
        half = self.rows(1, 0, 32, 32)
        self.b = go(half, half, self.zm)
        self.p.wait_recv()
        other = self.rows(0, 1)
        self.lp = go(other, other, self.zp)
        self.rp = go(other, other, self.zm)

    def far(self):
        go = self.net.go
        self.lp.wait_recv()
        half = self.rows(-1, 1, 0, 32)
        self.ha = go(half, half, self.zp)
        self.rp.wait_recv()
        half = self.rows(1, 1, 32, 32)
        self.hb = go(half, half, self.zm)

    def end(self):
        for copy in (self.a, self.b, self.ha, self.hb):
            copy.wait_recv()


def gather_kernel(
    x_ref, ct_ref, aw_ref, ew_ref, cw_ref, norm_ref,
    normed_ref, gb_ref, w_ref, norm_out,
    own_n, own_g, own_w, sums, landed, send, recv, local,
):
    at = place()
    z, xh, y, xl, c = at
    stages = stage_peers(at)
    net, near = Net(send, recv), Local(local)
    greet([peer for stage in stages for peer in stage])
    weights = [WeightGather(net, at, w_ref, kind) for kind in range(KINDS)]
    blocks = (aw_ref, ew_ref, cw_ref)
    kept = []

    def cast_own(kind):
        own_w[kind] = blocks[kind][...].astype(bf16)
        weights[kind].own(own_w.at[kind])
        kept.append(near.go(own_w.at[kind], weights[kind].rows(0, 0)))

    sums[0] = norm_ref[...]

    def between(stage):
        if stage == 1:
            cast_own(0)
            cast_own(1)

            @pl.loop(0, ROWS // 16)
            def _(i):
                part = pl.ds(i * 16, 16)
                own_g[part] = ct_ref[part].astype(bf16)

    staged_sum(net, stages, sums, landed, between)
    norm_out[...] = sums[4]
    gain, bias = spread(sums[4])

    @pl.loop(0, ROWS // 16)
    def _(i):
        part = pl.ds(i * 16, 16)
        x = x_ref[part]
        centred = x - jnp.mean(x, axis=1, keepdims=True)
        inverse = lax.rsqrt(jnp.mean(centred * centred, axis=1, keepdims=True) + eps_norm)
        own_n[part] = (centred * inverse * gain + bias).astype(bf16)

    normed = TokenGather(net, at, normed_ref)
    grads = TokenGather(net, at, gb_ref)
    normed.own(own_n)
    kept.append(near.go(own_n, normed.rows(0, 0)))
    weights[0].near()
    normed.near()
    grads.own(own_g)
    kept.append(near.go(own_g, grads.rows(0, 0)))
    weights[1].near()
    cast_own(2)
    weights[0].far()
    normed.far()
    weights[1].far()
    weights[2].near()
    normed.rest()
    grads.near()
    weights[2].far()
    grads.far()
    grads.rest()
    for item in weights + [normed, grads]:
        item.end()
    net.drain()
    for copy in kept:
        copy.wait()


def gather(x, ct, aw, ew, cw, norm_rows):
    any_ref = pl.BlockSpec(memory_space=pl.ANY)
    vmem = pl.BlockSpec(memory_space=pltpu.VMEM)
    return pl.pallas_call(
        gather_kernel,
        name="gather",
        out_shape=(
            jax.ShapeDtypeStruct((LENGTH, D), bf16),
            jax.ShapeDtypeStruct((LENGTH, D), bf16),
            jax.ShapeDtypeStruct((WALL, D), bf16),
            jax.ShapeDtypeStruct((8, 512), f32),
        ),
        in_specs=[vmem] * 6,
        out_specs=(any_ref, any_ref, any_ref, vmem),
        scratch_shapes=[
            pltpu.VMEM((ROWS, D), bf16),
            pltpu.VMEM((ROWS, D), bf16),
            pltpu.VMEM((KINDS, WROWS, D), bf16),
            pltpu.VMEM((5, 8, 512), f32),
            pltpu.VMEM((10, 8, 512), f32),
            pltpu.SemaphoreType.DMA((80,)),
            pltpu.SemaphoreType.DMA((80,)),
            pltpu.SemaphoreType.DMA((8,)),
        ],
        compiler_params=pltpu.CompilerParams(
            collective_id=1, has_side_effects=True, vmem_limit_bytes=48 << 20
        ),
    )(x, ct, aw, ew, cw, norm_rows)


def add_rows(count, put, *refs):
    @pl.loop(0, count // 16)
    def _(i):
        part = pl.ds(pl.multiple_of(i * 16, 16), 16)
        total = refs[0][part].astype(f32)
        for ref in refs[1:]:
            total = total + ref[part].astype(f32)
        put(part, total)


def add_into(count, out, *refs):
    def put(part, total):
        out[part] = total.astype(out.dtype)

    add_rows(count, put, *refs)


PLACES = [(0, 0), (-1, 0), (1, 0), (2, 0), (0, 1), (-1, 1), (1, 1), (2, 1)]


class TokenScatter:
    def __init__(self, net, near, at, part, mine, sibs, landed, out):
        self.net, self.near, self.at, self.part = net, near, at, part
        self.mine, self.sibs, self.landed, self.out = mine, sibs, landed, out
        z, xh, y, xl, c = at
        self.xpart = device(z, xh, y, 1 - xl, c)
        self.yp = device(z, xh, y + 1, xl, c)
        self.ym = device(z, xh, y - 1, xl, c)
        self.sib = device(z, xh, y, xl, 1 - c)
        self.loads, self.swaps = {}, {}

    def slot(self, dy, dx):
        return PLACES.index((dy, dx))

    def swap(self, dy, dx):
        z, xh, y, xl, c = self.at
        x, slot = (xl if dx == 0 else 1 - xl), self.slot(dy, dx)
        self.swaps[slot] = self.net.go(
            self.part.at[token_rows(y + dy, x, 1 - c)], self.sibs.at[slot], self.sib
        )
        self.loads[slot] = self.near.go(
            self.part.at[token_rows(y + dy, x, c)], self.mine.at[slot]
        )

    def swap_all(self):
        for dy, dx in ((2, 1), (-1, 1), (1, 1), (2, 0), (-1, 0), (1, 0), (0, 1), (0, 0)):
            self.swap(dy, dx)

    def ready(self, dy, dx, *more):
        slot = self.slot(dy, dx)
        self.loads[slot].wait()
        self.swaps[slot].wait_recv()
        add_into(ROWS, self.mine.at[slot], self.mine.at[slot], self.sibs.at[slot], *more)
        return self.mine.at[slot]

    def send(self, src, slot, peer, start=0, size=ROWS):
        return self.net.go(src, self.landed.at[slot, pl.ds(start, size)], peer)

    def far(self):
        self.xo = self.send(self.ready(2, 1), 0, self.xpart)
        self.lp = self.send(self.ready(-1, 1), 1, self.ym)
        self.rp = self.send(self.ready(1, 1), 2, self.yp)

    def opposite(self):
        self.xo.wait_recv()
        block = self.ready(2, 0, self.landed.at[0])
        self.a = self.send(block.at[pl.ds(0, 64)], 3, self.ym, 0, 64)
        self.b = self.send(block.at[pl.ds(64, 64)], 3, self.yp, 64, 64)

    def near_left(self):
        block = self.ready(-1, 0)
        self.a.wait_recv()
        top = pl.ds(0, 64)
        add_into(64, block.at[top], block.at[top], self.landed.at[3, top])
        self.l = self.send(block, 4, self.ym)

    def near_right(self):
        block = self.ready(1, 0)
        self.b.wait_recv()
        low = pl.ds(64, 64)
        add_into(64, block.at[low], block.at[low], self.landed.at[3, low])
        self.r = self.send(block, 5, self.yp)

    def partner(self):
        self.lp.wait_recv()
        self.rp.wait_recv()
        block = self.ready(0, 1, self.landed.at[1], self.landed.at[2])
        self.p = self.send(block, 6, self.xpart)

    def final(self):
        self.l.wait_recv()
        self.r.wait_recv()
        self.p.wait_recv()
        slot = self.slot(0, 0)
        self.loads[slot].wait()
        self.swaps[slot].wait_recv()
        add_into(
            ROWS, self.out, self.mine.at[slot], self.sibs.at[slot],
            self.landed.at[4], self.landed.at[5], self.landed.at[6],
        )


class WeightScatter:
    def __init__(self, net, at, part, kind, landed, out):
        self.net, self.at, self.part, self.kind = net, at, part, kind
        self.landed, self.out = landed, out
        z, xh, y, xl, c = at
        self.hpart = device(z, 1 - xh, y, xl, c)
        self.zp = device(z + 1, xh, y, xl, c)
        self.zm = device(z - 1, xh, y, xl, c)

    def rows(self, dz, dh, start=0, size=WROWS):
        z, xh = self.at[:2]
        return self.part.at[
            weight_rows(self.kind, z + dz, xh if dh == 0 else 1 - xh, start, size)
        ]

    def send(self, src, slot, peer, start=0, size=WROWS):
        return self.net.go(src, self.landed.at[slot, pl.ds(start, size)], peer)

    def opposite(self):
        self.a, self.b = [], []
        for dh in (0, 1):
            self.a.append(self.send(self.rows(2, dh, 0, 32), dh, self.zm, 0, 32))
            self.b.append(self.send(self.rows(2, dh, 32, 32), dh, self.zp, 32, 32))

    def near(self):
        self.l, self.r = [], []
        for dh in (1, 0):
            self.a[dh].wait_recv()
            half = self.rows(-1, dh, 0, 32)
            add_into(32, half, half, self.landed.at[dh, pl.ds(0, 32)])
            self.l.append(self.send(self.rows(-1, dh), 2 + dh, self.zm))
            self.b[dh].wait_recv()
            half = self.rows(1, dh, 32, 32)
            add_into(32, half, half, self.landed.at[dh, pl.ds(32, 32)])
            self.r.append(self.send(self.rows(1, dh), 4 + dh, self.zp))

    def partner(self):
        self.l[0].wait_recv()
        self.r[0].wait_recv()
        other = self.rows(0, 1)
        add_into(WROWS, other, other, self.landed.at[3], self.landed.at[5])
        self.p = self.send(other, 6, self.hpart)

    def final(self):
        self.l[1].wait_recv()
        self.r[1].wait_recv()
        self.p.wait_recv()
        add_into(
            WROWS, self.out, self.rows(0, 0),
            self.landed.at[2], self.landed.at[4], self.landed.at[6],
        )


def scatter_kernel(
    branch_ref, dnormed_ref, wgrad_ref,
    branch_out, dnormed_out, wgrad_out,
    mine, sibs, landed, wpart, wlanded, send, recv, local,
):
    at = place()
    z, xh, y, xl, c = at
    net, near = Net(send, recv), Local(local)
    greet(
        [
            device(z, xh, y, 1 - xl, c),
            device(z, xh, y, xl, 1 - c),
            device(z, xh, y + 1, xl, c),
            device(z, xh, y - 1, xl, c),
            device(z + 1, xh, y, xl, c),
            device(z - 1, xh, y, xl, c),
            device(z, 1 - xh, y, xl, c),
        ]
    )
    loads = {}
    for kind, (start, size) in ((2, (FIRST + 128, HIDDEN)), (1, (QKV, HIDDEN)), (0, (0, QKV))):
        loads[kind] = [near.go(wgrad_ref.at[pl.ds(start, size)], wpart.at[pl.ds(start, size)])]
    loads[0].append(near.go(wgrad_ref.at[pl.ds(FIRST, 128)], wpart.at[pl.ds(FIRST, 128)]))
    tokens = [
        TokenScatter(net, near, at, part, mine.at[k], sibs.at[k], landed.at[k], out)
        for k, (part, out) in enumerate(((branch_ref, branch_out), (dnormed_ref, dnormed_out)))
    ]
    weights = [
        WeightScatter(net, at, wpart, kind, wlanded.at[kind], wgrad_out.at[kind])
        for kind in range(KINDS)
    ]
    branch, dnormed = tokens
    branch.swap_all()
    for kind in (2, 1, 0):
        for load in loads[kind]:
            load.wait()
        weights[kind].opposite()
    dnormed.swap_all()
    branch.far()
    weights[2].near()
    branch.opposite()
    branch.near_left()
    branch.near_right()
    weights[1].near()
    dnormed.far()
    dnormed.opposite()
    weights[0].near()
    branch.partner()
    dnormed.near_left()
    dnormed.near_right()
    for kind in (2, 1, 0):
        weights[kind].partner()
    branch.final()
    dnormed.partner()
    for kind in (2, 1, 0):
        weights[kind].final()
    dnormed.final()
    net.drain()


def scatter(branch, dnormed, wgrad):
    any_ref = pl.BlockSpec(memory_space=pl.ANY)
    vmem = pl.BlockSpec(memory_space=pltpu.VMEM)
    return pl.pallas_call(
        scatter_kernel,
        name="scatter",
        out_shape=(
            jax.ShapeDtypeStruct((ROWS, D), f32),
            jax.ShapeDtypeStruct((ROWS, D), f32),
            jax.ShapeDtypeStruct((KINDS, WROWS, D), f32),
        ),
        in_specs=[any_ref] * 3,
        out_specs=(vmem,) * 3,
        scratch_shapes=[
            pltpu.VMEM((2, 8, ROWS, D), bf16),
            pltpu.VMEM((2, 8, ROWS, D), bf16),
            pltpu.VMEM((2, 7, ROWS, D), bf16),
            pltpu.VMEM((WALL, D), bf16),
            pltpu.VMEM((KINDS, 7, WROWS, D), bf16),
            pltpu.SemaphoreType.DMA((80,)),
            pltpu.SemaphoreType.DMA((80,)),
            pltpu.SemaphoreType.DMA((24,)),
        ],
        compiler_params=pltpu.CompilerParams(
            collective_id=2, has_side_effects=True, vmem_limit_bytes=58 << 20
        ),
    )(branch, dnormed, wgrad)


def norm_sum_kernel(part_ref, out_ref, sums, landed, send, recv):
    stages = stage_peers(place())
    net = Net(send, recv)
    greet([peer for stage in stages for peer in stage])
    sums[0] = part_ref[...]
    staged_sum(net, stages, sums, landed)
    out_ref[...] = sums[4]
    net.drain()


def norm_sum(part):
    vmem = pl.BlockSpec(memory_space=pltpu.VMEM)
    return pl.pallas_call(
        norm_sum_kernel,
        name="norm_sum",
        out_shape=jax.ShapeDtypeStruct((8, 512), f32),
        in_specs=[vmem],
        out_specs=vmem,
        scratch_shapes=[
            pltpu.VMEM((5, 8, 512), f32),
            pltpu.VMEM((10, 8, 512), f32),
            pltpu.SemaphoreType.DMA((10,)),
            pltpu.SemaphoreType.DMA((10,)),
        ],
        compiler_params=pltpu.CompilerParams(collective_id=3, has_side_effects=True),
    )(part)


def angles(positions, half):
    freq = rope_base ** (-2.0 * jnp.arange(half, dtype=jnp.float32) / (2 * half))
    turned = positions[:, None] * freq[None, :]
    return (jnp.cos(turned)[:, None, :], jnp.sin(turned)[:, None, :])


def rotate(values, cosine, sine):
    half = cosine.shape[-1]
    first = values[..., :half]
    second = values[..., half : 2 * half]
    return jnp.concatenate(
        [first * cosine - second * sine, second * cosine + first * sine, values[..., 2 * half :]],
        axis=-1,
    )


def gelu(values):
    return jax.nn.gelu(values, approximate=True)


def causal(offset, block, width):
    rows_at = offset + lax.broadcasted_iota(jnp.int32, (block, width), 0)
    cols_at = lax.broadcasted_iota(jnp.int32, (block, width), 1)
    return (cols_at <= rows_at)[None]


def block_scores(query, keys, start, block, first):
    stop = start + block
    scores = jnp.einsum(
        "qhe,khe->hqk", query[start:stop], keys[first:stop], preferred_element_type=jnp.float32
    ) * HD ** (-0.5)
    return jnp.where(causal(start - first, block, stop - first), scores, masked_score)


def attend_forward(whole, heads, block, seq_len):
    length = whole.shape[0]
    query = whole[:, 0].reshape(length, heads, HD)
    keys = whole[:, 1].reshape(length, heads, HD)
    value = whole[:, 2].reshape(length, heads, HD)
    outputs = []
    totals = []
    for index in range(length // block):
        start = index * block
        stop = start + block
        first = start // seq_len * seq_len
        scores = block_scores(query, keys, start, block, first)
        top = jnp.max(scores, axis=-1, keepdims=True)
        expo = jnp.exp(scores - top)
        total = jnp.sum(expo, axis=-1, keepdims=True)
        probs = (expo / total).astype(jnp.bfloat16)
        attended = jnp.einsum(
            "hqk,khe->qhe", probs, value[first:stop], preferred_element_type=jnp.float32
        )
        outputs.append(attended.astype(jnp.bfloat16).reshape(block, heads * HD))
        totals.append(top + jnp.log(total))
    return (jnp.concatenate(outputs, axis=0), totals)


def attend_backward(whole, totals, grad_attended, heads, block, seq_len):
    length = whole.shape[0]
    scale = HD ** (-0.5)
    query = whole[:, 0].reshape(length, heads, HD)
    keys = whole[:, 1].reshape(length, heads, HD)
    value = whole[:, 2].reshape(length, heads, HD)
    grad_out = grad_attended.reshape(length, heads, HD)
    grad_query = []
    grad_keys = jnp.zeros((length, heads, HD), jnp.float32)
    grad_value = jnp.zeros((length, heads, HD), jnp.float32)
    for index in range(length // block):
        start = index * block
        stop = start + block
        first = start // seq_len * seq_len
        scores = block_scores(query, keys, start, block, first)
        probs_full = jnp.exp(scores - totals[index])
        probs = probs_full.astype(jnp.bfloat16)
        grad_block = grad_out[start:stop]
        grad_value = grad_value.at[first:stop].add(
            jnp.einsum("hqk,qhe->khe", probs, grad_block, preferred_element_type=jnp.float32)
        )
        grad_probs = jnp.einsum(
            "qhe,khe->hqk", grad_block, value[first:stop], preferred_element_type=jnp.float32
        )
        inner = jnp.sum(probs_full * grad_probs, axis=-1, keepdims=True)
        grad_scores = (probs_full * (grad_probs - inner)).astype(jnp.bfloat16)
        grad_query.append(
            (
                jnp.einsum(
                    "hqk,khe->qhe",
                    grad_scores,
                    keys[first:stop],
                    preferred_element_type=jnp.float32,
                )
                * scale
            ).astype(jnp.bfloat16)
        )
        grad_keys = grad_keys.at[first:stop].add(
            jnp.einsum(
                "hqk,qhe->khe", grad_scores, query[start:stop], preferred_element_type=jnp.float32
            )
            * scale
        )
    stacked = [
        jnp.concatenate(grad_query, axis=0),
        grad_keys.astype(jnp.bfloat16),
        grad_value.astype(jnp.bfloat16),
    ]
    return jnp.stack([piece.reshape(length, heads * HD) for piece in stacked], axis=1)


def polish(moment):
    size = jnp.sqrt(jnp.sum(moment * moment, axis=(1, 2), keepdims=True)) + 1e-07
    current = moment / size

    def times(a, b):
        return jnp.einsum("bij,bjk->bik", a, b, precision=highest)

    gram = jnp.einsum("bij,bkj->bik", current, current, precision=highest)
    whole = jnp.eye(HD, dtype=f32)[None]
    for turn in range(NS_STEPS):
        factor = (
            polish_a * jnp.eye(HD, dtype=f32)[None] + polish_b * gram + polish_c * times(gram, gram)
        )
        whole = factor if turn == 0 else times(factor, whole)
        if turn < NS_STEPS - 1:
            gram = times(factor, times(gram, factor))
    return times(whole, current)


def body(
    inputs, cotangent, attn_weight, expand_weight, contract_weight, norm_params,
    attn_moment, expand_moment, contract_moment, norm_first, norm_second,
):
    index = (lax.axis_index("fsdp") * 8 + lax.axis_index("seq")) * 4 + lax.axis_index("mp")
    mine = (jnp.arange(D, dtype=jnp.int32) // 16) == index
    norm_rows = jnp.where(mine[None], jnp.tile(norm_params[0], (1, 128)), 0.0).reshape(8, 512)
    normed, grad_group, weights, norm_rows = gather(
        inputs,
        cotangent,
        attn_weight[0, 0],
        expand_weight[0],
        contract_weight[0],
        norm_rows,
    )
    gain = norm_rows.reshape(2, D)[0]
    first_w, second_w = weights[:FIRST], weights[FIRST:]
    cosine, sine = angles(jnp.arange(LENGTH, dtype=f32), ROT // 2)
    lin = lax.dot_general(normed, first_w[:QKV], across, preferred_element_type=f32)
    upward = lax.dot_general(normed, first_w[QKV:], across, preferred_element_type=f32)
    lin = lin.reshape(LENGTH, 3, 2, HD)
    query = rotate(lin[:, 0], cosine, sine).astype(bf16)
    keys = rotate(lin[:, 1], cosine, sine).astype(bf16)
    value = lin[:, 2].astype(bf16)
    whole = jnp.stack([query, keys, value], axis=1).reshape(LENGTH, 3, 2 * HD)
    attended, totals = attend_forward(whole, 2, 512, LENGTH)
    active = gelu(upward).astype(bf16)
    inner = jnp.concatenate([attended, active], axis=1)
    branch = jnp.dot(inner, second_w, preferred_element_type=f32).astype(bf16)
    grad_inner = lax.dot_general(grad_group, second_w, across, preferred_element_type=f32)
    grad_attended = grad_inner[:, :128].astype(bf16)
    slope = jax.vjp(gelu, upward)[1]
    grad_up = slope(grad_inner[:, 128:])[0].astype(bf16)
    second_part = lax.dot_general(inner, grad_group, downward, preferred_element_type=f32)
    grad_whole = attend_backward(whole, totals, grad_attended, 2, 512, LENGTH)
    grad_query = rotate(
        grad_whole[:, 0].reshape(LENGTH, 2, HD).astype(f32), cosine, -sine
    ).astype(bf16)
    grad_keys = rotate(
        grad_whole[:, 1].reshape(LENGTH, 2, HD).astype(f32), cosine, -sine
    ).astype(bf16)
    outer = jnp.concatenate(
        [
            grad_query.reshape(LENGTH, 128),
            grad_keys.reshape(LENGTH, 128),
            grad_whole[:, 2],
            grad_up,
        ],
        axis=1,
    )
    first_part = lax.dot_general(outer, normed, downward, preferred_element_type=f32)
    grad_normed = jnp.dot(outer, first_w, preferred_element_type=f32).astype(bf16)
    parts = jnp.concatenate([first_part, second_part], axis=0).astype(bf16)
    branch, hidden_gradient, shares = scatter(branch, grad_normed, parts)

    state = inputs + branch
    feature_mean = jnp.mean(inputs, axis=-1, keepdims=True)
    centered_input = inputs - feature_mean
    inverse_deviation = lax.rsqrt(
        jnp.mean(centered_input * centered_input, axis=-1, keepdims=True) + eps_norm
    )
    normalized_input = centered_input * inverse_deviation
    norm_part = jnp.stack(
        [jnp.sum(hidden_gradient * normalized_input, axis=0), jnp.sum(hidden_gradient, axis=0)],
        axis=0,
    )
    scaled = hidden_gradient * gain
    grad_state = cotangent + inverse_deviation * (
        scaled
        - jnp.mean(scaled, axis=-1, keepdims=True)
        - normalized_input * jnp.mean(scaled * normalized_input, axis=-1, keepdims=True)
    )
    norm_total = norm_sum(norm_part.reshape(8, 512)).reshape(2, D)
    norm_share = lax.dynamic_slice(norm_total, (0, index * 16), (2, 16))[None]

    moments = jnp.stack([attn_moment[0, 0], expand_moment[0], contract_moment[0]])
    moments = muon_beta * moments + shares
    ortho = polish(moments)
    updates = []
    for k, weight in enumerate((attn_weight, expand_weight, contract_weight)):
        shape = weight.shape
        new = weight - muon_rate * (
            muon_decay * weight + 0.2 * math.sqrt(D) * ortho[k].reshape(shape)
        )
        updates += [shares[k].reshape(shape), moments[k].reshape(shape), new]
    first_next = adam_first * norm_first + (1.0 - adam_first) * norm_share
    second_next = adam_second * norm_second + (1.0 - adam_second) * norm_share * norm_share
    first_fix = 1.0 - adam_first**STEP
    second_fix = 1.0 - adam_second**STEP
    norm_next = norm_params - adam_rate * (first_next / first_fix) / (
        jnp.sqrt(second_next / second_fix) + adam_eps
    )
    return (state, grad_state, *updates, norm_share, first_next, second_next, norm_next)


def solution(mesh):
    return jax.shard_map(
        body,
        mesh=mesh,
        in_specs=(
            P(("fsdp", "seq", "mp"), None),
            P(("fsdp", "seq", "mp"), None),
            P(None, ("fsdp", "seq", "mp"), None, None),
            P(None, ("fsdp", "seq", "mp"), None),
            P(None, ("fsdp", "seq", "mp"), None),
            P(None, None, ("fsdp", "seq", "mp")),
            P(None, ("fsdp", "seq", "mp"), None, None),
            P(None, ("fsdp", "seq", "mp"), None),
            P(None, ("fsdp", "seq", "mp"), None),
            P(None, None, ("fsdp", "seq", "mp")),
            P(None, None, ("fsdp", "seq", "mp")),
        ),
        out_specs=(
            P(("fsdp", "seq", "mp"), None),
            P(("fsdp", "seq", "mp"), None),
            P(None, ("fsdp", "seq", "mp"), None, None),
            P(None, ("fsdp", "seq", "mp"), None, None),
            P(None, ("fsdp", "seq", "mp"), None, None),
            P(None, ("fsdp", "seq", "mp"), None),
            P(None, ("fsdp", "seq", "mp"), None),
            P(None, ("fsdp", "seq", "mp"), None),
            P(None, ("fsdp", "seq", "mp"), None),
            P(None, ("fsdp", "seq", "mp"), None),
            P(None, ("fsdp", "seq", "mp"), None),
            P(None, None, ("fsdp", "seq", "mp")),
            P(None, None, ("fsdp", "seq", "mp")),
            P(None, None, ("fsdp", "seq", "mp")),
            P(None, None, ("fsdp", "seq", "mp")),
        ),
        check_vma=False,
    )
```

time: 1920 us -> 363 us (0.19)
  waiting for transfers between devices: 1390 us -> 0 us
  Pallas kernels: 0 us -> 199 us
  blocking collectives: 197 us -> 0 us
  local copies, waits for them, and re-layouts: 87.7 us -> 9.01 us
  matrix products: 160 us -> 121 us
    unnamed x12 -> x0, waiting for transfers between devices: 623 us -> none
    reduce_scatter x5 -> x0, waiting for transfers between devices: 575 us -> none  [the longest x1 197 us: body(): lax.psum_scatter(contract_part.astype(jnp.bfloat16), ('fsdp', 'seq'), sca...]
    pallas_call x0 -> x3, Pallas kernels: none -> 199 us  [the longest x1 94 us: gather(): pl.pallas_call(gather_kernel, name='gather', out_shape=(jax.ShapeDtypeStr...]
    all_gather x1 -> x0, blocking collectives: 197 us -> none  [body(): lax.all_gather(norm_params, ('fsdp', 'seq', 'mp'), axis=2, tiled=True)]
    all_gather x5 -> x0, waiting for transfers between devices: 178 us -> none  [the longest x1 105 us: body(): lax.all_gather(expand_weight[layer_module].astype(jnp.bfloat16), ('fsdp',...]
    slice x6 -> x5, local copies, waits for them, and re-layouts: 41.3 us -> 2.43 us  [the longest x2 2.35 us: body(): updates += [shares[k].reshape(shape), moments[k].reshape(shape), new]]
    unnamed x117 -> x92, local copies, waits for them, and re-layouts: 26.4 us -> 3.34 us
    dot_general x42 -> x25, matrix products: 106 us -> 86.2 us  [the longest x1 14 us: body(): lax.dot_general(inner, grad_group, downward, preferred_element_type=f32)]
  transfers between devices with their start and end apart: 15 -> 0, of which waited for: 10 -> 0; matrix products, arithmetic and copies ran while one was open for 13% -> 0% of each run, Pallas kernels for 0% -> 0%
where the time goes in v1:
time: 363 us; the launch traced here: 358 us
  Pallas kernels  199 us (55%)
  matrix products  121 us (33%)
  other arithmetic  27.9 us (8%)
  local copies, waits for them, and re-layouts  9.01 us (2%)
    pallas_call x1, Pallas kernels, gather(): pl.pallas_call(gather_kernel, name='gather', out_shape=(jax.ShapeDtypeStr...  94 us
    pallas_call x1, Pallas kernels, scatter(): pl.pallas_call(scatter_kernel, name='scatter', out_shape=(jax.ShapeDtypeS...  89.1 us
    pallas_call x1, Pallas kernels, norm_sum(): pl.pallas_call(norm_sum_kernel, name='norm_sum', out_shape=jax.ShapeDtype...  15.4 us
    dot_general x1, matrix products, body(): lax.dot_general(inner, grad_group, downward, preferred_element_type=f32)  14 us
    dot_general x1, matrix products, body(): jnp.dot(outer, first_w, preferred_element_type=f32).astype(bf16)  13.5 us
    dot_general x1, matrix products, body(): branch = jnp.dot(inner, second_w, preferred_element_type=f32).astype(bf16)  13.5 us
    dot_general x1, matrix products, body(): lax.dot_general(normed, first_w[QKV:], across, preferred_element_type=f32)  11.9 us
    dot_general x1, matrix products, body(): lax.dot_general(grad_group, second_w, across, preferred_element_type=f32)  11.1 us

profile of v1, /device:TPU:0, one launch (start us, length us, event | category | flops | bytes accessed | tf_op | source)
XLA Modules:
  0.0 358.3 jit_solution(16769596728014621057)
XLA Ops:
  9.7 94.0 %gather.1 = (bf16[2048,2048]{1,0:T(8,128)(2,1)}, bf16[2048,2048]{1,0:T(8,128)(2,1)}, bf16[1536,2048]{1,0:T(8,128)(2,1)}, f32[8,512]{1,0:T(8,128)S(1)}) custom-call(f32[128,2048]{1,0:T(8,128)S(1)} %copy-done, f32[128,2048]{1,0:T(8,128)S(1)} %copy-done.1, f32[64,2048]{1,0:T(8,128)S(1)} %bitcast.247, f32[64,2048]{1,0:T(8,128)S(1)} %bitcast.248, ...), custom_call_target="tpu_custom_call" | custom-call | tf_op jit(solution)/shard_map/gather/pallas_call | solution.py:333
  104.3 6.3 %fusion.58 = f32[2048,384]{0,1:T(8,128)S(1)} fusion(bf16[2048,2048]{1,0:T(8,128)(2,1)} %get-tuple-element.134, bf16[1536,2048]{1,0:T(8,128)(2,1)} %get-tuple-element.135), kind=kOutput, calls=%fused_computation.84 | convolution fusion | flops 3221225472 | bytes 13107200 | tf_op jit(solution)/shard_map/dot_general | solution.py:778
  115.7 1.7 fusion.77
  120.0 2.5 fusion.78
  122.6 2.0 fusion.129
  125.8 2.7 fusion.79
  128.5 11.1 %fusion.133 = (bf16[2048,640]{0,1:T(8,128)(2,1)S(1)}, f32[2048,640]{0,1:T(8,128)}) fusion(bf16[2048,2048]{1,0:T(8,128)(2,1)} %get-tuple-element.136, bf16[1536,2048]{1,0:T(8,128)(2,1)} %get-tuple-element.135), kind=kOutput, calls=%fused_computation.230 | convolution fusion | flops 5370019840 | bytes 18874368 | tf_op jit(solution)/shard_map/dot_general | solution.py:789
  141.2 1.8 fusion.31
  143.0 2.3 fusion.42
  148.0 2.1 multiply_reduce_fusion.2
  153.2 11.9 %fusion.10 = (bf16[2048,512]{0,1:T(8,128)(2,1)}, bf16[2048,512]{0,1:T(8,128)(2,1)S(1)}) fusion(f32[2048,640]{0,1:T(8,128)} %get-tuple-element.192, bf16[2048,2048]{1,0:T(8,128)(2,1)} %get-tuple-element.134, bf16[1536,2048]{1,0:T(8,128)(2,1)} %get-tuple-element.135), kind=kOutput, calls=%fused_computation.27 | convolution fusion | flops 4318035968 | bytes 18874368 | tf_op jit(solution)/shard_map/dot_general | solution.py:779
  165.2 14.0 %convolution_convert_fusion.3 = bf16[640,2048]{1,0:T(8,128)(2,1)} fusion(bf16[2048,2048]{1,0:T(8,128)(2,1)} %get-tuple-element.136, bf16[2048,512]{0,1:T(8,128)(2,1)S(1)} %get-tuple-element.151, bf16[512,128]{0,1:T(8,128)(2,1)S(1)} %bitcast.278, bf16[512,128]{0,1:T(8,128)(2,1)S(1)} %bitcast.276, bf16[512,128]{0,1:T(8,128)(2,1)S(1)} %bitcast.274, ...), kind=kOutput, calls=%fused_computation.44 | convolution fusion | flops 5383127040 | bytes 13631488 | tf_op jit(solution)/shard_map/dot_general | solution.py:793
  179.2 1.8 multiply_reduce_fusion.1
  184.2 2.2 multiply_reduce_fusion
  186.4 1.9 multiply_convert_fusion
  192.6 10.5 %convolution_convert_fusion.2 = bf16[896,2048]{1,0:T(8,128)(2,1)S(1)} fusion(bf16[2048,2048]{1,0:T(8,128)(2,1)} %get-tuple-element.134, bf16[2048,512]{0,1:T(8,128)(2,1)S(1)} %copy-done.44, bf16[2048,128]{0,1:T(8,128)(2,1)S(1)} %bitcast.261, bf16[2048,128]{0,1:T(8,128)(2,1)S(1)} %bitcast.263, bf16[2048,128]{0,1:T(8,128)(2,1)S(1)} %bitcast.265), kind=kOutput, calls=%fused_computation.42 | convolution fusion | flops 7532707840 | bytes 15728640 | tf_op jit(solution)/shard_map/dot_general | solution.py:810
  203.2 3.2 pad_maximum_fusion.wgrad_ref
  206.4 13.5 %convolution_convert_fusion.dnormed_ref = bf16[2048,2048]{1,0:T(8,128)(2,1)} fusion(bf16[1536,2048]{1,0:T(8,128)(2,1)} %get-tuple-element.135, bf16[2048,512]{0,1:T(8,128)(2,1)} %get-tuple-element.150, bf16[2048,128]{0,1:T(8,128)(2,1)S(1)} %bitcast.262, bf16[2048,128]{0,1:T(8,128)(2,1)S(1)} %bitcast.264, bf16[2048,128]{0,1:T(8,128)(2,1)S(1)} %bitcast.266), kind=kOutput, calls=%fused_computation.6 | convolution fusion | flops 7535067136 | bytes 15728640 | tf_op jit(solution)/shard_map/dot_general | solution.py:811
  219.9 13.5 %convolution_convert_fusion.1.branch_ref = bf16[2048,2048]{1,0:T(8,128)(2,1)} fusion(bf16[1536,2048]{1,0:T(8,128)(2,1)} %get-tuple-element.135, bf16[2048,512]{0,1:T(8,128)(2,1)S(1)} %copy-done.43, bf16[512,128]{0,1:T(8,128)(2,1)S(1)} %bitcast.279, bf16[512,128]{0,1:T(8,128)(2,1)S(1)} %bitcast.277, bf16[512,128]{0,1:T(8,128)(2,1)S(1)} %bitcast.275, ...), kind=kOutput, calls=%fused_computation.7 | convolution fusion | flops 5386010624 | bytes 13631488 | tf_op jit(solution)/shard_map/dot_general | solution.py:788
  233.4 89.1 %scatter.1 = (f32[128,2048]{1,0:T(8,128)}, f32[128,2048]{1,0:T(8,128)}, f32[3,64,2048]{2,1,0:T(8,128)}) custom-call(bf16[2048,2048]{1,0:T(8,128)(2,1)} %convolution_convert_fusion.1.branch_ref, bf16[2048,2048]{1,0:T(8,128)(2,1)} %convolution_convert_fusion.dnormed_ref, bf16[1536,2048]{1,0:T(8,128)(2,1)} %pad_maximum_fusion.wgrad_ref), custom_call_target="tpu_custom_call" | custom-call | tf_op jit(solution)/shard_map/scatter/pallas_call | solution.py:578
  322.5 1.7 multiply_reduce_fusion.5
  324.9 15.4 %norm_sum.1 = f32[8,512]{1,0:T(8,128)} custom-call(f32[8,512]{1,0:T(8,128)} %reshape.597.part_ref), custom_call_target="tpu_custom_call" | custom-call | tf_op jit(solution)/shard_map/norm_sum/pallas_call | solution.py:616
  341.1 3.5 multiply_add_fusion
  347.5 1.7 fusion.106
  (185 shorter events, 45.8 us)
Async XLA Ops:
  0.6 8.0 %copy-start = (f32[128,2048]{1,0:T(8,128)S(1)}, f32[128,2048]{1,0:T(8,128)}, u32[]{:S(2)}) copy-start(f32[128,2048]{1,0:T(8,128)} %x_ref.1) | copy-start | bytes 3145732
  110.9 34.5 %copy-start.7 = (bf16[2048,3,2,64]{0,3,2,1:T(8,128)(2,1)}, bf16[2048,3,2,64]{0,3,2,1:T(8,128)(2,1)S(1)}, u32[]{:S(2)}) copy-start(bf16[2048,3,2,64]{0,3,2,1:T(8,128)(2,1)S(1)} %convert.41) | copy-start | bytes 4718596
  111.3 11.3 %copy-start.15 = (bf16[2048,1,2,16]{0,3,2,1:T(8,128)(2,1)}, bf16[2048,1,2,16]{0,3,2,1:T(8,128)(2,1)S(1)}, u32[]{:S(2)}) copy-start(bf16[2048,1,2,16]{0,3,2,1:T(8,128)(2,1)S(1)} %get-tuple-element.172) | copy-start | bytes 393220
  111.3 11.3 %copy-start.17 = (bf16[2048,1,2,16]{0,3,2,1:T(8,128)(2,1)}, bf16[2048,1,2,16]{0,3,2,1:T(8,128)(2,1)S(1)}, u32[]{:S(2)}) copy-start(bf16[2048,1,2,16]{0,3,2,1:T(8,128)(2,1)S(1)} %get-tuple-element.173) | copy-start | bytes 393220
  111.3 36.1 %copy-start.10 = (bf16[2048,1,2,64]{0,3,2,1:T(8,128)(2,1)}, bf16[2048,1,2,64]{0,3,2,1:T(8,128)(2,1)S(1)}, u32[]{:S(2)}) copy-start(bf16[2048,1,2,64]{0,3,2,1:T(8,128)(2,1)S(1)} %pad_maximum_fusion.5) | copy-start | bytes 1572868
  153.2 12.0 %copy-start.34 = (bf16[2,64,512]{2,1,0:T(8,128)(2,1)S(1)}, bf16[2,64,512]{2,1,0:T(8,128)(2,1)}, u32[]{:S(2)}) copy-start(bf16[2,64,512]{2,1,0:T(8,128)(2,1)} %convolution_convert_fusion.4) | copy-start | bytes 393220
  153.2 12.0 %copy-start.36 = (bf16[2,64,512]{2,1,0:T(8,128)(2,1)S(1)}, bf16[2,64,512]{2,1,0:T(8,128)(2,1)}, u32[]{:S(2)}) copy-start(bf16[2,64,512]{2,1,0:T(8,128)(2,1)} %fusion.77) | copy-start | bytes 393220
  153.2 12.0 %copy-start.38 = (bf16[2,64,512]{2,1,0:T(8,128)(2,1)S(1)}, bf16[2,64,512]{2,1,0:T(8,128)(2,1)}, u32[]{:S(2)}) copy-start(bf16[2,64,512]{2,1,0:T(8,128)(2,1)} %fusion.78) | copy-start | bytes 393220
  153.2 12.0 %copy-start.40 = (bf16[2,64,512]{2,1,0:T(8,128)(2,1)S(1)}, bf16[2,64,512]{2,1,0:T(8,128)(2,1)}, u32[]{:S(2)}) copy-start(bf16[2,64,512]{2,1,0:T(8,128)(2,1)} %fusion.79) | copy-start | bytes 393220
  165.2 14.0 %copy-start.42 = (bf16[2048,512]{0,1:T(8,128)(2,1)}, bf16[2048,512]{0,1:T(8,128)(2,1)S(1)}, u32[]{:S(2)}) copy-start(bf16[2048,512]{0,1:T(8,128)(2,1)S(1)} %get-tuple-element.151) | copy-start | bytes 6291460
  165.2 14.0 %copy-start.8 = (bf16[2048,3,2,64]{0,3,2,1:T(8,128)(2,1)S(1)}, bf16[2048,3,2,64]{0,3,2,1:T(8,128)(2,1)}, u32[]{:S(2)}) copy-start(bf16[2048,3,2,64]{0,3,2,1:T(8,128)(2,1)} %copy-done.7) | copy-start | bytes 4718596
  165.2 14.0 %copy-start.13 = (bf16[512,128]{0,1:T(8,128)(2,1)S(1)}, bf16[512,128]{0,1:T(8,128)(2,1)}, u32[]{:S(2)}) copy-start(bf16[512,128]{0,1:T(8,128)(2,1)} %copy-done.12) | copy-start | bytes 393220
  192.6 10.6 %copy-start.9 = (bf16[640,2048]{1,0:T(8,128)(2,1)S(1)}, bf16[640,2048]{1,0:T(8,128)(2,1)}, u32[]{:S(2)}) copy-start(bf16[640,2048]{1,0:T(8,128)(2,1)} %convolution_convert_fusion.3) | copy-start | bytes 7864324
  206.3 13.5 %copy-start.35 = (bf16[2,64,512]{2,1,0:T(8,128)(2,1)S(1)}, bf16[2,64,512]{2,1,0:T(8,128)(2,1)}, u32[]{:S(2)}) copy-start(bf16[2,64,512]{2,1,0:T(8,128)(2,1)} %convolution_convert_fusion.4) | copy-start | bytes 393220
  206.3 13.5 %copy-start.37 = (bf16[2,64,512]{2,1,0:T(8,128)(2,1)S(1)}, bf16[2,64,512]{2,1,0:T(8,128)(2,1)}, u32[]{:S(2)}) copy-start(bf16[2,64,512]{2,1,0:T(8,128)(2,1)} %fusion.77) | copy-start | bytes 393220
  206.3 13.5 %copy-start.39 = (bf16[2,64,512]{2,1,0:T(8,128)(2,1)S(1)}, bf16[2,64,512]{2,1,0:T(8,128)(2,1)}, u32[]{:S(2)}) copy-start(bf16[2,64,512]{2,1,0:T(8,128)(2,1)} %fusion.78) | copy-start | bytes 393220
  206.3 13.6 %copy-start.41 = (bf16[2,64,512]{2,1,0:T(8,128)(2,1)S(1)}, bf16[2,64,512]{2,1,0:T(8,128)(2,1)}, u32[]{:S(2)}) copy-start(bf16[2,64,512]{2,1,0:T(8,128)(2,1)} %fusion.79) | copy-start | bytes 393220
  206.4 13.5 %copy-start.43 = (bf16[2048,512]{0,1:T(8,128)(2,1)S(1)}, bf16[2048,512]{0,1:T(8,128)(2,1)}, u32[]{:S(2)}) copy-start(bf16[2048,512]{0,1:T(8,128)(2,1)} %copy-done.42) | copy-start | bytes 6291460
  233.4 89.1 %copy-start.27 = (f32[1,4,4,128]{3,1,2,0:T(4,128)S(1)}, f32[1,4,4,128]{3,1,2,0:T(4,128)}, u32[]{:S(2)}) copy-start(f32[1,4,4,128]{3,1,2,0:T(4,128)} %copy.38) | copy-start | bytes 24580
  233.4 89.1 %copy-start.29 = (f32[128]{0:T(128)S(1)}, f32[128]{0:T(128)}, u32[]{:S(2)}) copy-start(f32[128]{0:T(128)} %copy-done.28) | copy-start | bytes 1540
  233.4 89.1 %copy-start.31 = (f32[128]{0:T(128)S(1)}, f32[128]{0:T(128)}, u32[]{:S(2)}) copy-start(f32[128]{0:T(128)} %add_rsqrt_fusion) | copy-start | bytes 1540
  322.5 22.7 %copy-start.30 = (f32[1,2,16]{2,1,0:T(2,128)S(1)}, f32[1,2,16]{2,1,0:T(2,128)}, u32[]{:S(2)}) copy-start(f32[1,2,16]{2,1,0:T(2,128)} %param.36) | copy-start | bytes 388
  322.5 22.7 %copy-start.32 = (f32[1,2,16]{2,1,0:T(2,128)S(1)}, f32[1,2,16]{2,1,0:T(2,128)}, u32[]{:S(2)}) copy-start(f32[1,2,16]{2,1,0:T(2,128)} %param.41) | copy-start | bytes 388
  322.5 22.7 %copy-start.33 = (f32[1,2,16]{2,1,0:T(2,128)S(1)}, f32[1,2,16]{2,1,0:T(2,128)}, u32[]{:S(2)}) copy-start(f32[1,2,16]{2,1,0:T(2,128)} %param.40) | copy-start | bytes 388
  (21 other events, 72.8 us)
